TPU v7x, 256 devices: a whole 4x4x8 slice. The times are simulated.
256 devices in a mesh: ma: 32 (over z, y), freq: 8 (over x, core).
Axes of the slice: x: 4, y: 4, z: 8, core: 2. Of those that a mesh axis runs over, the one named last changes fastest.
Arguments:
- visibilities: bfloat16 [512, 32, 4, 512], P('ma', 'freq'), may hold values from -6 to 6
- transfer: bfloat16 [32, 64, 512, 1024], P('freq', 'ma'), may hold values from -1 to 1, as said below
- noise_weight: float32 [32, 512], P('freq'), may hold values from 1 to 12, as said below
- freq_prior: float32 [32, 32], P('freq'), may hold values from -1 to 5, as said below
Outputs:
- sky_map: float32 [32, 64, 4, 1024], P('freq', 'ma')
- residual: float32 [32, 64, 4, 1024], P('freq', 'ma')
- direction: float32 [32, 64, 4, 1024], P('freq', 'ma')
Inputs may be any that keep to these rules, and one draw needn't show every extreme that they name: Real transfer blocks of the m-modes in the window. `noise_weight`: positive weights. `freq_prior`: symmetric positive definite.
All inputs are finite; a program needn't handle non-finite values.
Results may differ from a plain program's by a relative error of at most 0.0056.
Values may be sent and summed in bfloat16 or wider, within the bound.
A program may use at most 64 MiB of HBM per device.

v0:
```python
import math

import jax
import jax.numpy as jnp
from jax import lax
from jax.sharding import PartitionSpec as P


def harmonic_lookup(harmonic_number, leading_epoch, epoch_number, whole_epoch_grid):
    harmonic_slot = jnp.arange(harmonic_number, dtype=jnp.int32)
    observing_epochs = leading_epoch + jnp.arange(epoch_number, dtype=jnp.int32)
    rotation_argument = harmonic_slot[:, None] * observing_epochs[None, :] % whole_epoch_grid
    rotation_radians = rotation_argument.astype(jnp.float32) * (2.0 * math.pi / whole_epoch_grid)
    return (
        (jnp.cos(rotation_radians) + jnp.sin(rotation_radians))
        * (1.0 / math.sqrt(whole_epoch_grid))
    ).astype(jnp.bfloat16)


def local(visibilities, transfer, noise_weight, freq_prior):
    epochs_each_shard, frequency_per_device, realization_count, baseline_pairs = visibilities.shape
    harmonics_each_shard = transfer.shape[1]
    harmonic_amount = lax.axis_size("ma")
    whole_epoch_grid = epochs_each_shard * harmonic_amount
    column_total = frequency_per_device * realization_count * baseline_pairs
    flat_vis = visibilities.reshape(epochs_each_shard, column_total)
    leading_epoch = lax.axis_index("ma") * epochs_each_shard
    cas_rows = harmonic_lookup(
        harmonics_each_shard * lax.axis_size("ma"),
        leading_epoch,
        epochs_each_shard,
        whole_epoch_grid,
    )
    mode_totals = lax.psum_scatter(
        jnp.dot(cas_rows, flat_vis, preferred_element_type=jnp.float32),
        "ma",
        scatter_dimension=0,
        tiled=True,
    )
    visibility_modes = mode_totals.reshape(
        harmonics_each_shard, frequency_per_device, realization_count, baseline_pairs
    )
    weighted = (noise_weight[None, :, None, :] * visibility_modes).astype(jnp.bfloat16)
    right_side = jnp.einsum(
        "fmbs,mfkb->fmks", transfer, weighted, preferred_element_type=jnp.float32
    )
    right_low = right_side.astype(jnp.bfloat16)
    observed = jnp.einsum(
        "fmbs,fmks->fmkb", transfer, right_low, preferred_element_type=jnp.float32
    )
    scaled = (noise_weight[:, None, None, :] * observed).astype(jnp.bfloat16)
    adjoint = jnp.einsum("fmbs,fmkb->fmks", transfer, scaled, preferred_element_type=jnp.float32)
    coupled = jnp.einsum(
        "fg,gmks->fmks",
        freq_prior,
        lax.all_gather(right_side, "freq", axis=0, tiled=True),
        precision=lax.Precision.HIGHEST,
    )
    applied = adjoint + coupled
    local_norm = jnp.sum(right_side * right_side, axis=(0, 1, 3))
    local_curve = jnp.sum(right_side * applied, axis=(0, 1, 3))
    norm_now = lax.psum(local_norm, ("ma", "freq"))
    curvature = lax.psum(local_curve, ("ma", "freq"))
    step_plain = norm_now / curvature
    residual = right_side - step_plain[None, None, :, None] * applied
    norm_next = lax.psum(jnp.sum(residual * residual, axis=(0, 1, 3)), ("ma", "freq"))
    sky_map = step_plain[None, None, :, None] * right_side
    direction = residual + (norm_next / norm_now)[None, None, :, None] * right_side
    return (sky_map, residual, direction)


def solution(mesh):
    return jax.shard_map(
        local,
        mesh=mesh,
        in_specs=(
            P("ma", "freq", None, None),
            P("freq", "ma", None, None),
            P("freq", None),
            P("freq", None),
        ),
        out_specs=(
            P("freq", "ma", None, None),
            P("freq", "ma", None, None),
            P("freq", "ma", None, None),
        ),
        check_vma=False,
    )
```

profile of v0, /device:TPU:1, one launch (start us, length us, event | category | flops | bytes accessed | tf_op | source)
XLA Modules:
  0.0 370.0 jit_solution(2050857011195431761)
XLA Ops:
  7.2 0.0 copy-start
  7.2 0.0 copy-start.2
  7.2 0.0 all-reduce.4.cloned.1.call-start
  7.2 1.1 reshape.20
  8.4 1.9 fusion.16
  10.3 0.0 all-reduce.4.cloned.1.call-update
  10.3 0.0 all-gather.2.cloned.1.call-start
  10.3 1.3 dynamic-slice
  12.3 153.0 %all-reduce.4.cloned.1.call-done = f32[64,8192]{1,0:T(8,128)} async-done(((f32[64,8192]{1,0:T(8,128)}), f32[64,8192]{1,0:T(8,128)}) %all-reduce.4.cloned.1.call-update) | async-done | bytes 2097168
  165.3 1.0 constant_dynamic-slice_fusion
  166.3 0.1 reshape.21
  166.3 5.3 %fusion.6 = f32[4,2,4,1024]{3,2,1,0:T(4,128)} fusion(bf16[4,2,512,1024]{3,2,1,0:T(8,128)(2,1)} %param.5, f32[2,4,4,512]{3,2,1,0:T(4,128)S(1)} %reshape.21, f32[4,512]{1,0:T(4,128)} %param.6), kind=kOutput, calls=%fused_computation.14 | convolution fusion | flops 33587200 | bytes 8593408 | tf_op jit(solution)/shard_map/fmbs,mfkb->fmks/dot_general | solution.py:44
  171.6 0.0 all-gather.2.cloned.1.call-update
  171.6 27.8 %all-gather.2.cloned.1.call-done = f32[32,2,4,1024]{3,2,1,0:T(4,128)} async-done(((f32[4,2,4,1024]{3,2,1,0:T(4,128)}), f32[32,2,4,1024]{3,2,1,0:T(4,128)}) %all-gather.2.cloned.1.call-update) | async-done | bytes 1048592 | tf_op jit(solution)/shard_map/all_gather | solution.py:56
  199.4 0.0 copy-done
  199.4 2.4 fusion.1
  201.8 0.0 copy-done.2
  201.8 0.0 copy-start.1
  201.8 9.3 %multiply_reduce_fusion.1 = (f32[4]{0:T(128)S(1)}, f32[4]{0:T(128)S(1)}, f32[4,2,4,1024]{3,2,1,0:T(4,128)S(1)}) fusion(f32[4,2,4,1024]{3,2,1,0:T(4,128)} %fusion.6, f32[2,4,1024,4]{2,3,1,0:T(4,128)S(1)} %fusion.1, bf16[4,2,512,1024]{3,2,1,0:T(8,128)(2,1)} %param.5, f32[4,512]{1,0:T(4,128)S(1)} %copy-done.2), kind=kOutput, calls=%fused_computation.8 | convolution fusion | flops 67338240 | bytes 8790048 | tf_op jit(solution)/shard_map/fmbs,fmkb->fmks/dot_general | solution.py:52
  211.2 76.0 %all-reduce.1 = (f32[4]{0:T(128)S(1)}, f32[4]{0:T(128)S(1)}) all-reduce(f32[4]{0:T(128)S(1)} %get-tuple-element.4, f32[4]{0:T(128)S(1)} %get-tuple-element.3), channel_id=1, replica_groups=mesh['ma'=32,'freq'=8] {'ma','freq'}, use_global_device_ids=true, to_apply=%region_2.3 | all-reduce | flops 8 | bytes 64 | tf_op jit(solution)/shard_map/psum | solution.py:62
  287.2 0.0 copy-done.1
  287.2 0.9 multiply_reduce_fusion
  288.1 0.0 copy-start.3
  288.1 74.3 %psum.23 = f32[4]{0:T(128)S(1)} all-reduce(f32[4]{0:T(128)S(1)} %get-tuple-element.7), channel_id=1, replica_groups=mesh['ma'=32,'freq'=8] {'ma','freq'}, use_global_device_ids=true, to_apply=%region_6.7 | all-reduce | flops 4 | bytes 32 | tf_op jit(solution)/shard_map/psum | solution.py:66
  362.4 0.8 multiply_add_fusion
  363.1 0.0 copy-done.3
  (3 shorter events, 0.0 us)
Async XLA Ops:
  7.2 192.2 %copy-start = (f32[4,32]{1,0:T(4,128)S(1)}, f32[4,32]{1,0:T(4,128)}, u32[]{:S(2)}) copy-start(f32[4,32]{1,0:T(4,128)} %param.7) | copy-start | bytes 1540
  7.2 194.6 %copy-start.2 = (f32[4,512]{1,0:T(4,128)S(1)}, f32[4,512]{1,0:T(4,128)}, u32[]{:S(2)}) copy-start(f32[4,512]{1,0:T(4,128)} %param.6) | copy-start | bytes 24580
  7.2 158.1 %all-reduce.4.cloned.1.call-start = ((), (), s32[]{:S(2)}) async-start(), calls=%async_computation.1 | async-start | bytes 4194304
  10.3 189.1 %all-gather.2.cloned.1.call-start = ((), (), s32[]{:S(2)}) async-start(), calls=%async_computation | async-start | bytes 1179648 | tf_op jit(solution)/shard_map/all_gather | solution.py:56
  201.8 85.4 %copy-start.1 = (f32[4,2,4,1024]{3,2,1,0:T(4,128)S(1)}, f32[4,2,4,1024]{3,2,1,0:T(4,128)}, u32[]{:S(2)}) copy-start(f32[4,2,4,1024]{3,2,1,0:T(4,128)} %fusion.6) | copy-start | bytes 393220
  288.1 75.0 %copy-start.3 = (f32[4,2,4,1024]{3,2,1,0:T(4,128)}, f32[4,2,4,1024]{3,2,1,0:T(4,128)S(1)}, u32[]{:S(2)}) copy-start(f32[4,2,4,1024]{3,2,1,0:T(4,128)S(1)} %get-tuple-element.8) | copy-start | bytes 393220
Sparse Core Ops, SparseCore 0:
  11.5 153.6 all-reduce.3
  171.7 27.6 all-gather.1
where the time goes:
time: 370 us
  waiting for transfers between devices  181 us (49%)
  blocking collectives  150 us (41%)
  matrix products  18.9 us (5%)
  between operations  14.8 us (4%)
    unnamed x3, waiting for transfers between devices  153 us
    psum x1, blocking collectives, local(): norm_now = lax.psum(local_norm, ('ma', 'freq'))  76 us
    psum x1, blocking collectives, local(): lax.psum(jnp.sum(residual * residual, axis=(0, 1, 3)), ('ma', 'freq'))  74.3 us
    all_gather x1, waiting for transfers between devices, local(): lax.all_gather(right_side, 'freq', axis=0, tiled=True)  27.8 us
    dot_general x1, matrix products, local(): jnp.einsum('fmbs,fmkb->fmks', transfer, scaled, preferred_element_type=jn...  9.35 us
  transfers between devices with their start and end apart: 2, of which 2 were waited for; matrix products, arithmetic and copies ran while one was open for 0% of the time, Pallas kernels for 0%

commit v1 on v0

v1 whole, which is shorter than its diff:
```python
import math

import jax
import jax.numpy as jnp
import numpy as np
from jax import lax
from jax.experimental import pallas as pl
from jax.experimental.pallas import tpu as pltpu
from jax.sharding import PartitionSpec as P

NZ, NY, NX, NC = 8, 4, 4, 2
NF, NM, NB, NS, SIMS, NT, TL = 4, 2, 512, 1024, 4, 512, 16
ROWS = NM * SIMS
F32, BF16 = jnp.float32, jnp.bfloat16
HIGH = lax.Precision.HIGHEST


def cas_table():
    m = np.arange(64)
    t = np.arange(NT)
    arg = (m[:, None] * t[None, :]) % NT
    ang = arg.astype(np.float32) * np.float32(2.0 * math.pi / NT)
    cas = (np.cos(ang) + np.sin(ang)) * np.float32(1.0 / math.sqrt(NT))
    cas = cas.reshape(64, NZ, 64).transpose(1, 0, 2)
    eye = np.eye(SIMS, dtype=np.float32)
    full = cas[:, :, None, :, None] * eye[None, None, :, None, :]
    return full.reshape(NZ, 256, 256).astype(jnp.bfloat16)


def dot(a, b, **kw):
    return jnp.dot(a, b, preferred_element_type=F32, **kw)


def dot_t(a, b):
    return lax.dot_general(a, b, (((1,), (1,)), ((), ())), preferred_element_type=F32)


def kernel(vis, transfer, weight, prior, cas, right_out, applied_out, coef_out,
           tv, casv, vbuf, pbuf, rbuf, right, adj, rall, sib_out, sib_in, prior_sib, dsend, d1, d2,
           tsem, lsem, ps, a1s, a1r, a2s, a2r, cs, cr, ss, sr, d1s, d1r, d2s, d2r):
    ma = lax.axis_index("ma")
    fq = lax.axis_index("freq")
    z, y = ma // NY, ma % NY
    x, c = fq // NC, fq % NC

    def ma_peer(dz, dy):
        return lax.rem(z + dz, NZ) * NY + lax.rem(y + dy, NY)

    def fq_peer(dx, dc):
        return lax.rem(x + dx, NX) * NC + lax.rem(c + dc, NC)

    ma_offsets = [(dz, dy) for dz in range(NZ) for dy in range(NY) if dz or dy]
    fq_offsets = [(dx, dc) for dx in range(NX) for dc in range(NC) if dx or dc]

    tcopies = [pltpu.make_async_copy(transfer.at[f], tv.at[f], tsem.at[f]) for f in range(NF)]
    cas_copy = pltpu.make_async_copy(cas.at[z], casv, lsem.at[0])
    own_vis = pltpu.make_async_copy(vis.at[y], vbuf.at[y], lsem.at[1])
    cas_copy.start()
    own_vis.start()

    barrier = pltpu.get_barrier_semaphore()
    for dz, dy in ma_offsets:
        pl.semaphore_signal(barrier, 1, device_id={"ma": ma_peer(dz, dy), "freq": fq})
    for dx, dc in fq_offsets:
        pl.semaphore_signal(barrier, 1, device_id={"ma": ma, "freq": fq_peer(dx, dc)})
    pl.semaphore_wait(barrier, len(ma_offsets) + len(fq_offsets))

    a1 = []
    for dy in range(1, NY):
        a1.append(pltpu.make_async_remote_copy(
            vis.at[lax.rem(y + dy, NY)], vbuf.at[y], a1s.at[dy - 1], a1r.at[dy - 1],
            device_id={"ma": ma_peer(0, dy), "freq": fq}))
        a1[-1].start()
    pc = pltpu.make_async_remote_copy(prior, prior_sib, ps.at[0], ps.at[1],
                                      device_id={"ma": ma, "freq": fq_peer(0, 1)})
    pc.start()
    for t in tcopies:
        t.start()

    pc.wait()

    def spread(p):
        i0 = lax.broadcasted_iota(jnp.int32, (NF * ROWS, NF), 0)
        i1 = lax.broadcasted_iota(jnp.int32, (NF * ROWS, NF), 1)
        e1 = (i0 // ROWS == i1).astype(F32)
        j0 = lax.broadcasted_iota(jnp.int32, (32, NX * NF * ROWS), 0)
        j1 = lax.broadcasted_iota(jnp.int32, (32, NX * NF * ROWS), 1)
        g = (j1 // 32) * 8 + c * 4 + (j1 // 8) % 4
        e2 = (j0 == g).astype(F32)
        k0 = lax.broadcasted_iota(jnp.int32, (NF * ROWS, NX * NF * ROWS), 0)
        k1 = lax.broadcasted_iota(jnp.int32, (NF * ROWS, NX * NF * ROWS), 1)
        full = dot(dot(e1, p, precision=HIGH), e2, precision=HIGH)
        return jnp.where(k0 % ROWS == k1 % ROWS, full, 0.0)

    pri = jnp.concatenate([spread(prior[...]), spread(prior_sib[...])], axis=0)
    pri_hi = pri.astype(BF16)
    pri_lo = (pri - pri_hi.astype(F32)).astype(BF16)
    pri_all = jnp.concatenate([pri_hi, pri_lo], axis=0)

    cas_copy.wait()
    own_vis.wait()
    for r in a1:
        r.wait()

    part = dot(casv[...], vbuf[...].reshape(256, NB)).reshape(32, ROWS, NB)
    pbuf[...] = jnp.concatenate([part[:, :, :256], part[:, :, 256:]], axis=1).astype(BF16)
    a2 = []
    for dz, dy in ma_offsets:
        slot = dz * NY + dy - 1
        peer = ma_peer(dz, dy)
        a2.append(pltpu.make_async_remote_copy(
            pbuf.at[peer], rbuf.at[slot], a2s, a2r, device_id={"ma": peer, "freq": fq}))
        a2[-1].start()
    for t in tcopies:
        t.wait()
    rcv = pltpu.make_async_copy(rbuf, rbuf, a2r)
    rcv.wait()

    row = lax.broadcasted_iota(jnp.int32, (ROWS, 1), 0)
    low = row < SIMS

    def both(a, f, form):
        return jnp.where(low, form(a, tv[f, 0]), form(a, tv[f, 1]))

    for dy in range(NY):
        f = lax.rem(y + NY - dy, NY)
        total = None
        for dz in range(NZ):
            slot = dz * NY + dy
            piece = pbuf[ma] if slot == 0 else rbuf[slot - 1]
            piece = piece.astype(F32)
            total = piece if total is None else total + piece
        modes = jnp.concatenate([total[:ROWS], total[ROWS:]], axis=1)
        weighted = (weight[pl.ds(f, 1), :] * modes).astype(BF16)
        right[f] = both(weighted, f, dot)

    rall[x] = right[...].reshape(NF * ROWS, NS).astype(BF16)
    cc = []
    for dx in range(1, NX):
        cc.append(pltpu.make_async_remote_copy(
            rall.at[x], rall.at[x], cs.at[dx - 1], cr.at[dx - 1],
            device_id={"ma": ma, "freq": fq_peer(dx, 0)}))
        cc[-1].start()

    for f in range(NF):
        observed = both(right[f].astype(BF16), f, dot_t)
        scaled = (weight[pl.ds(f, 1), :] * observed).astype(BF16)
        adj[f] = both(scaled, f, dot)

    for r in cc:
        r.wait()
    cp = dot(pri_all, rall[...].reshape(NX * NF * ROWS, NS))
    cp = cp[:64] + cp[64:]
    sib_out[...] = cp[32:].astype(BF16)
    sc = pltpu.make_async_remote_copy(sib_out, sib_in, ss, sr,
                                      device_id={"ma": ma, "freq": fq_peer(0, 1)})
    sc.start()
    part_applied = adj[...].reshape(NF * ROWS, NS) + cp[:32]
    sc.wait()
    applied = (part_applied + sib_in[...].astype(F32)).reshape(NF, ROWS, NS)
    rt = right[...]
    applied_out[...] = applied
    right_out[...] = rt

    def rows(v):
        return jnp.sum(jnp.sum(v, axis=0), axis=1, keepdims=True)

    lane = lax.broadcasted_iota(jnp.int32, (ROWS, 128), 1)
    n, cu, q = rows(rt * rt), rows(rt * applied), rows(applied * applied)
    own = jnp.where(lane == 0, n, jnp.where(lane == 1, cu, jnp.where(lane == 2, q, 0.0)))
    dsend[0] = own
    dd = []
    for i, (dz, dy) in enumerate(ma_offsets):
        dd.append(pltpu.make_async_remote_copy(
            dsend.at[0], d1.at[i], d1s, d1r, device_id={"ma": ma_peer(dz, dy), "freq": fq}))
        dd[-1].start()
    pltpu.make_async_copy(d1, d1, d1r).wait()
    own = own + jnp.sum(d1[...], axis=0)
    dsend[1] = own
    de = []
    for i, (dx, dc) in enumerate(fq_offsets):
        de.append(pltpu.make_async_remote_copy(
            dsend.at[1], d2.at[i], d2s, d2r, device_id={"ma": ma, "freq": fq_peer(dx, dc)}))
        de[-1].start()
    pltpu.make_async_copy(d2, d2, d2r).wait()
    coef_out[...] = own + jnp.sum(d2[...], axis=0)
    for r in a2 + dd + de:
        r.wait_send()


def local(visibilities, transfer, noise_weight, freq_prior):
    vis = visibilities.transpose(1, 0, 2, 3).reshape(NF, TL * SIMS, NB)
    vm = pl.BlockSpec(memory_space=pltpu.VMEM)
    hbm = pl.BlockSpec(memory_space=pl.ANY)
    dma = pltpu.SemaphoreType.DMA
    out = jax.ShapeDtypeStruct((NF, ROWS, NS), F32)
    right, applied, sums = pl.pallas_call(
        kernel,
        out_shape=(out, out, jax.ShapeDtypeStruct((ROWS, 128), F32)),
        in_specs=[hbm, hbm, vm, vm, hbm],
        out_specs=(vm, vm, vm),
        scratch_shapes=[
            pltpu.VMEM((NF, NM, NB, NS), BF16),
            pltpu.VMEM((256, 256), BF16),
            pltpu.VMEM((NY, TL * SIMS, NB), BF16),
            pltpu.VMEM((32, 16, 256), BF16),
            pltpu.VMEM((31, 16, 256), BF16),
            pltpu.VMEM((NF, ROWS, NS), F32),
            pltpu.VMEM((NF, ROWS, NS), F32),
            pltpu.VMEM((NX, NF * ROWS, NS), BF16),
            pltpu.VMEM((NF * ROWS, NS), BF16),
            pltpu.VMEM((NF * ROWS, NS), BF16),
            pltpu.VMEM((NF, 32), F32),
            pltpu.VMEM((2, ROWS, 128), F32),
            pltpu.VMEM((31, ROWS, 128), F32),
            pltpu.VMEM((7, ROWS, 128), F32),
            dma((NF,)), dma((2,)), dma((2,)), dma((3,)), dma((3,)), dma, dma, dma((3,)), dma((3,)),
            dma, dma, dma, dma, dma, dma,
        ],
        compiler_params=pltpu.CompilerParams(
            collective_id=0, has_side_effects=True, vmem_limit_bytes=40 * 1024 * 1024),
    )(vis, transfer, noise_weight, freq_prior, jnp.asarray(cas_table()))
    sums = sums[:SIMS, :3] + sums[SIMS:, :3]
    norm, curve, image = sums[:, 0], sums[:, 1], sums[:, 2]
    step = norm / curve
    ratio = (image / curve) * step - 1.0
    right = right.reshape(NF, NM, SIMS, NS)
    applied = applied.reshape(NF, NM, SIMS, NS)
    step, ratio = step[:, None], ratio[:, None]
    residual = right - step * applied
    return step * right, residual, residual + ratio * right


def solution(mesh):
    return jax.shard_map(
        local,
        mesh=mesh,
        in_specs=(
            P("ma", "freq", None, None),
            P("freq", "ma", None, None),
            P("freq", None),
            P("freq", None),
        ),
        out_specs=(P("freq", "ma", None, None),) * 3,
        check_vma=False,
    )
```

time: 370 us -> 54.3 us (0.15)
  waiting for transfers between devices: 181 us -> 0 us
  blocking collectives: 150 us -> 0 us
  Pallas kernels: 0 us -> 45.1 us
  matrix products: 18.9 us -> 0 us
  between operations: 14.8 us -> 0.68 us
    unnamed x3 -> x0, waiting for transfers between devices: 153 us -> none
    psum x2 -> x0, blocking collectives: 150 us -> none  [the longest x1 76 us: local(): norm_now = lax.psum(local_norm, ('ma', 'freq'))]
    pallas_call x0 -> x1, Pallas kernels: none -> 45.1 us  [local(): pl.pallas_call(kernel, out_shape=(out, out, jax.ShapeDtypeStruct((ROWS, 1...]
    all_gather x1 -> x0, waiting for transfers between devices: 27.8 us -> none  [local(): lax.all_gather(right_side, 'freq', axis=0, tiled=True)]
    dot_general x4 -> x0, matrix products: 18.9 us -> none  [the longest x1 9.35 us: local(): jnp.einsum('fmbs,fmkb->fmks', transfer, scaled, preferred_element_type=jn...]
    unnamed x10 -> x8, local copies, waits for them, and re-layouts: 2.27 us -> 5.98 us
  transfers between devices with their start and end apart: 2 -> 0, of which waited for: 2 -> 0; matrix products, arithmetic and copies ran while one was open for 0% -> 0% of each run, Pallas kernels for 0% -> 0%
where the time goes in v1:
time: 54.3 us; the launch traced here: 54 us
  Pallas kernels  45.1 us (83%)
  local copies, waits for them, and re-layouts  7.17 us (13%)
  other arithmetic  1.11 us (2%)
  between operations  0.68 us (1%)
    pallas_call x1, Pallas kernels, local(): pl.pallas_call(kernel, out_shape=(out, out, jax.ShapeDtypeStruct((ROWS, 1...  45.1 us
    unnamed x8, local copies, waits for them, and re-layouts  5.98 us

profile of v1, /device:TPU:1, one launch (start us, length us, event | category | flops | bytes accessed | tf_op | source)
XLA Modules:
  0.0 54.0 jit_solution(9878063587711347299)
XLA Ops:
  0.6 1.0 %copy.9 = bf16[4,16,4,512]{3,2,1,0:T(4,128)(2,1)S(1)} copy(bf16[4,16,4,512]{3,2,0,1:T(4,128)(2,1)} %bitcast.1) | data formatting | bytes 524288 | tf_op jit(solution)/shard_map/transpose | solution.py:192
  1.7 0.1 reshape.42.vis
  1.7 0.0 copy-start
  1.8 3.4 %copy-done = bf16[4,2,512,1024]{3,2,1,0:T(8,128)(2,1)S(1)} copy-done((bf16[4,2,512,1024]{3,2,1,0:T(8,128)(2,1)S(1)}, bf16[4,2,512,1024]{3,2,1,0:T(8,128)(2,1)}, u32[]{:S(2)}) %copy-start) | copy-done | bytes 8388632
  5.1 0.0 copy-start.1
  5.1 1.2 %copy-done.1 = bf16[8,256,256]{2,1,0:T(8,128)(2,1)S(1)} copy-done((bf16[8,256,256]{2,1,0:T(8,128)(2,1)S(1)}, bf16[8,256,256]{2,1,0:T(8,128)(2,1)}, u32[]{:S(2)}) %copy-start.1) | copy-done | bytes 1048600
  6.4 0.0 copy-start.2
  6.4 0.7 %copy-done.2 = f32[4,512]{1,0:T(4,128)S(1)} copy-done((f32[4,512]{1,0:T(4,128)S(1)}, f32[4,512]{1,0:T(4,128)}, u32[]{:S(2)}) %copy-start.2) | copy-done | bytes 8216
  7.1 0.0 copy-start.3
  7.1 0.7 %copy-done.3 = f32[4,32]{1,0:T(4,128)S(1)} copy-done((f32[4,32]{1,0:T(4,128)S(1)}, f32[4,32]{1,0:T(4,128)}, u32[]{:S(2)}) %copy-start.3) | copy-done | bytes 536
  7.7 45.1 %shard_map.76 = (f32[4,8,1024]{2,1,0:T(8,128)S(1)}, f32[4,8,1024]{2,1,0:T(8,128)S(1)}, f32[8,128]{1,0:T(8,128)S(1)}) custom-call(bf16[4,64,512]{2,1,0:T(8,128)(2,1)S(1)} %reshape.42.vis, bf16[4,2,512,1024]{3,2,1,0:T(8,128)(2,1)S(1)} %copy-done, f32[4,512]{1,0:T(4,128)S(1)} %copy-done.2, f32[4,32]{1,0:T(4,128)S(1)} %copy-done.3, ...), custom_call_target="tpu_custom_call" | custom-call | tf_op jit(solution)/shard_map/pallas_call | solution.py:197
  52.8 0.2 fusion.1
  53.2 0.9 %multiply_add_fusion = (f32[4,2,4,1024]{3,2,1,0:T(4,128)}, f32[4,2,4,1024]{3,2,1,0:T(4,128)}, f32[4,2,4,1024]{3,2,1,0:T(4,128)}) fusion(f32[4,2,4,1024]{3,2,1,0:T(4,128)S(1)} %reshape.43, f32[4]{0:T(128)S(1)} %multiply_add_fusion.1, f32[4,2,4,1024]{3,2,1,0:T(4,128)S(1)} %reshape.44, f32[4]{0:T(128)S(1)} %get-tuple-element.10), kind=kLoop, calls=%fused_computation | loop fusion | flops 163840 | bytes 655392 | tf_op jit(solution)/shard_map/add | solution.py:231
  (4 shorter events, 0.1 us)
Async XLA Ops:
  1.7 3.4 %copy-start = (bf16[4,2,512,1024]{3,2,1,0:T(8,128)(2,1)S(1)}, bf16[4,2,512,1024]{3,2,1,0:T(8,128)(2,1)}, u32[]{:S(2)}) copy-start(bf16[4,2,512,1024]{3,2,1,0:T(8,128)(2,1)} %transfer.1) | copy-start | bytes 25165828
  5.1 1.2 %copy-start.1 = (bf16[8,256,256]{2,1,0:T(8,128)(2,1)S(1)}, bf16[8,256,256]{2,1,0:T(8,128)(2,1)}, u32[]{:S(2)}) copy-start(bf16[8,256,256]{2,1,0:T(8,128)(2,1)} %constant.5.clone.cas) | copy-start | bytes 3145732
  6.4 0.7 %copy-start.2 = (f32[4,512]{1,0:T(4,128)S(1)}, f32[4,512]{1,0:T(4,128)}, u32[]{:S(2)}) copy-start(f32[4,512]{1,0:T(4,128)} %weight.1) | copy-start | bytes 24580
  7.1 0.7 %copy-start.3 = (f32[4,32]{1,0:T(4,128)S(1)}, f32[4,32]{1,0:T(4,128)}, u32[]{:S(2)}) copy-start(f32[4,32]{1,0:T(4,128)} %prior.1) | copy-start | bytes 1540

commit v2 on v0

v2 whole, which is shorter than its diff:
```python
import math

import jax
import jax.numpy as jnp
import numpy as np
from jax import lax
from jax.experimental import pallas as pl
from jax.experimental.pallas import tpu as pltpu
from jax.sharding import PartitionSpec as P

NZ, NY, NX, NC = 8, 4, 4, 2
NFQ = NX * NC
NF, NM, NB, NS, SIMS, NT, TL = 4, 2, 512, 1024, 4, 512, 16
F = NF * NFQ
ROWS = NM * SIMS
OWN = NF * ROWS
LANES = NS // NFQ
HALF = NB // 2
F32, BF16 = jnp.float32, jnp.bfloat16
HIGH = lax.Precision.HIGHEST
MA_OFFSETS = [(dz, dy) for dz in range(NZ) for dy in range(NY) if dz or dy]
FQ_OFFSETS = [(dx, dc) for dx in range(NX) for dc in range(NC) if dx or dc]


def cas_table():
    m = np.arange(64)
    t = np.arange(NT)
    arg = (m[:, None] * t[None, :]) % NT
    ang = arg.astype(np.float32) * np.float32(2.0 * math.pi / NT)
    cas = (np.cos(ang) + np.sin(ang)) * np.float32(1.0 / math.sqrt(NT))
    cas = cas.reshape(64, NZ, 64).transpose(1, 0, 2)
    eye = np.eye(SIMS, dtype=np.float32)
    full = cas[:, :, None, :, None] * eye[None, None, :, None, :]
    return full.reshape(NZ, 256, 256).astype(jnp.bfloat16)


def dot(a, b, **kw):
    return jnp.dot(a, b, preferred_element_type=F32, **kw)


def dot_t(a, b):
    return lax.dot_general(a, b, (((1,), (1,)), ((), ())), preferred_element_type=F32)


def iota(shape, dim):
    return lax.broadcasted_iota(jnp.int32, shape, dim)


def lane_tiles(v):
    v = sum(v[i * ROWS:(i + 1) * ROWS] for i in range(NF))
    return sum(v[:, i * 128:(i + 1) * 128] for i in range(NS // 128))


def kernel(vis, transfer, weight_hbm, prior_hbm, cas, right_out, applied_out, coef_out,
           tv, gram, casv, vbuf, pbuf, rbuf, right, adj, rsl, rin, asl, ain, csl, cin, prior, spread, weight, dsend, d1, d2,
           tsem, lsem, ps, pr, a1s, a1r, a2s, a2r, rs, rr, as_, ar, cs, cr, d1s, d1r, d2s, d2r):
    ma = lax.axis_index("ma")
    fq = lax.axis_index("freq")
    z, y = ma // NY, ma % NY
    x, c = fq // NC, fq % NC

    def ma_peer(dz, dy):
        return lax.rem(z + dz, NZ) * NY + lax.rem(y + dy, NY)

    def fq_peer(dx, dc):
        return lax.rem(x + dx, NX) * NC + lax.rem(c + dc, NC)

    def to_ma(dz, dy):
        return {"ma": ma_peer(dz, dy), "freq": fq}

    def to_fq(dx, dc):
        return {"ma": ma, "freq": fq_peer(dx, dc)}

    tcopies = [pltpu.make_async_copy(transfer.at[f], tv.at[f], tsem.at[f]) for f in range(NF)]
    halves = [pl.ds(h * HALF, HALF) for h in range(2)]
    cas_copy = pltpu.make_async_copy(cas.at[z], casv, lsem.at[0])
    own_vis = [pltpu.make_async_copy(vis.at[:, y, :, halves[h]], vbuf.at[h, y], lsem.at[1 + h]) for h in range(2)]
    own_prior = pltpu.make_async_copy(prior_hbm, prior.at[fq], lsem.at[3])
    own_weight = pltpu.make_async_copy(weight_hbm, weight, lsem.at[4])
    local_copies = [*own_vis, cas_copy, own_prior, own_weight]
    for t in local_copies:
        t.start()

    barrier = pltpu.get_barrier_semaphore()
    for o in MA_OFFSETS:
        pl.semaphore_signal(barrier, 1, device_id=to_ma(*o))
    for o in FQ_OFFSETS:
        pl.semaphore_signal(barrier, 1, device_id=to_fq(*o))
    pl.semaphore_wait(barrier, len(MA_OFFSETS) + len(FQ_OFFSETS))
    pending = []

    def send(src, dst, ssem, rsem, peer):
        copy = pltpu.make_async_remote_copy(src, dst, ssem, rsem, device_id=peer)
        copy.start()
        pending.append(copy)
        return copy

    a1 = [[send(vis.at[:, lax.rem(y + dy, NY), :, halves[h]], vbuf.at[h, y], a1s.at[h, dy - 1], a1r.at[h, dy - 1],
                to_ma(0, dy)) for dy in range(1, NY)] for h in range(2)]
    pcs = [send(prior_hbm, prior.at[fq], ps.at[i], pr.at[i], to_fq(*o)) for i, o in enumerate(FQ_OFFSETS)]
    for t in tcopies:
        t.start()
    cas_copy.wait()

    for h in range(2):
        own_vis[h].wait()
        for r in a1[h]:
            r.wait_recv()
        part = dot(casv[...], vbuf[h].reshape(256, HALF)).reshape(32, ROWS, HALF)
        pbuf[h] = jnp.concatenate([part[:, :, :128], part[:, :, 128:]], axis=1).astype(BF16)
        for dz, dy in MA_OFFSETS:
            send(pbuf.at[h, ma_peer(dz, dy)], rbuf.at[h, dz * NY + dy - 1], a2s, a2r.at[h], to_ma(dz, dy))

    own_prior.wait()
    own_weight.wait()
    for r in pcs:
        r.wait_recv()
    e1 = (iota((F * ROWS, F), 0) // ROWS == iota((F * ROWS, F), 1)).astype(F32)
    e2 = (iota((F, F * ROWS), 0) == iota((F, F * ROWS), 1) // ROWS).astype(F32)
    full = dot(dot(e1, prior[...].reshape(F, F), precision=HIGH), e2, precision=HIGH)
    same = iota((F * ROWS, F * ROWS), 0) % ROWS == iota((F * ROWS, F * ROWS), 1) % ROWS
    full = jnp.where(same, full, 0.0)
    spread[0] = full.astype(BF16)
    spread[1] = (full - full.astype(BF16).astype(F32)).astype(BF16)
    for t in tcopies:
        t.wait()

    @pl.loop(0, NF)
    def _(f):
        for m in range(NM):
            block = tv[f, m]
            gram[f, m] = dot_t(block, block).astype(BF16)

    low = iota((ROWS, 1), 0) < SIMS

    def both(a, ref, f, at=slice(None)):
        return jnp.where(low, dot(a, ref[f, 0, at]), dot(a, ref[f, 1, at]))

    acc, obs = [None] * NY, [None] * NY
    for h in range(2):
        pltpu.make_async_copy(rbuf.at[h], rbuf.at[h], a2r.at[h]).wait()
        for dy in range(NY):
            f = lax.rem(y + NY - dy, NY)
            total = None
            for dz in range(NZ):
                slot = dz * NY + dy
                piece = pbuf[h, ma] if slot == 0 else rbuf[h, slot - 1]
                piece = piece.astype(F32)
                total = piece if total is None else total + piece
            modes = jnp.concatenate([total[:ROWS], total[ROWS:]], axis=1)
            weighted = (weight[pl.ds(f, 1), halves[h]] * modes).astype(BF16)
            out = both(weighted, tv, f, halves[h])
            acc[dy] = out if h == 0 else acc[dy] + out
            out = both(weighted, gram, f, halves[h])
            obs[dy] = out if h == 0 else obs[dy] + out
    for dy in range(NY):
        right[lax.rem(y + NY - dy, NY)] = acc[dy]

    def slices(v, ref):
        v = v.astype(BF16)
        for j in range(NFQ):
            ref[j] = v[:, j * LANES:(j + 1) * LANES]

    rt = right[...].reshape(OWN, NS)
    slices(rt, rsl)
    rc = [send(rsl.at[fq_peer(*o)], rin.at[fq], rs.at[i], rr.at[i], to_fq(*o)) for i, o in enumerate(FQ_OFFSETS)]
    rin[fq] = rsl[fq]

    for dy in range(NY):
        f = lax.rem(y + NY - dy, NY)
        scaled = (weight[pl.ds(f, 1), :] * obs[dy]).astype(BF16)
        adj[f] = both(scaled, tv, f)
    at = adj[...].reshape(OWN, NS)
    slices(at, asl)
    ac = [send(asl.at[fq_peer(*o)], ain.at[fq], as_.at[i], ar.at[i], to_fq(*o)) for i, o in enumerate(FQ_OFFSETS)]
    ain[fq] = asl[fq]

    for r in rc:
        r.wait_recv()
    rall = rin[...].reshape(F * ROWS, LANES)
    coupled = dot(spread[...].reshape(2 * F * ROWS, F * ROWS), rall)
    coupled = coupled[:F * ROWS] + coupled[F * ROWS:]
    csl[...] = coupled.reshape(NFQ, OWN, LANES)
    cc = [send(csl.at[fq_peer(*o)], cin.at[fq], cs.at[i], cr.at[i], to_fq(*o)) for i, o in enumerate(FQ_OFFSETS)]
    cin[fq] = csl[fq]

    def blocks(v):
        return sum(v[i * ROWS:(i + 1) * ROWS] for i in range(F))

    n = lane_tiles(rt * rt)
    cu = lane_tiles(rt * at) + blocks(rall.astype(F32) * coupled)
    q = lane_tiles(at * at)
    for r in ac:
        r.wait_recv()
    q = q + blocks((2.0 * ain[...].reshape(F * ROWS, LANES).astype(F32) + coupled) * coupled)

    row, lane = iota((ROWS, 128), 0), iota((ROWS, 128), 1)

    def put(v, at_lane):
        return jnp.where(lane == row + at_lane, jnp.sum(v, axis=1, keepdims=True), 0.0)

    own = jnp.sum(put(n, 0) + put(cu, ROWS) + put(q, 2 * ROWS), axis=0, keepdims=True)
    dsend[0] = own
    for i, o in enumerate(MA_OFFSETS):
        send(dsend.at[0], d1.at[i], d1s, d1r, to_ma(*o))
    for f in range(NF):
        for m in range(NM):
            right_out[f, m] = right[f, m * SIMS:(m + 1) * SIMS]
    pltpu.make_async_copy(d1, d1, d1r).wait()
    own = own + jnp.sum(d1[...], axis=0)
    dsend[1] = own
    for i, o in enumerate(FQ_OFFSETS):
        send(dsend.at[1], d2.at[i], d2s, d2r, to_fq(*o))
    for r in cc:
        r.wait_recv()
    for f in range(NF):
        coup = jnp.concatenate([cin[j, f * ROWS:(f + 1) * ROWS] for j in range(NFQ)], axis=1)
        applied = adj[f] + coup
        for m in range(NM):
            applied_out[f, m] = applied[m * SIMS:(m + 1) * SIMS]
    pltpu.make_async_copy(d2, d2, d2r).wait()
    own = own + jnp.sum(d2[...], axis=0)

    def take(at_lane):
        inside = (lane >= at_lane) & (lane < at_lane + ROWS) & (lane % SIMS == row % SIMS)
        return jnp.sum(jnp.where(inside, own, 0.0), axis=1, keepdims=True)

    norm, curve, image = take(0), take(ROWS), take(2 * ROWS)
    step = norm / curve
    ratio = (image / curve) * step - 1.0
    coef_out[0] = jnp.broadcast_to(step[:SIMS], (SIMS, 128))
    coef_out[1] = jnp.broadcast_to(ratio[:SIMS], (SIMS, 128))
    for r in pending:
        r.wait_send()


def local(visibilities, transfer, noise_weight, freq_prior):
    vm = pl.BlockSpec(memory_space=pltpu.VMEM)
    hbm = pl.BlockSpec(memory_space=pltpu.HBM)
    dma = pltpu.SemaphoreType.DMA
    out = jax.ShapeDtypeStruct((NF, NM, SIMS, NS), F32)
    slab = pltpu.VMEM((NFQ, OWN, LANES), BF16)
    wide = pltpu.VMEM((NFQ, OWN, LANES), F32)
    right, applied, coef = pl.pallas_call(
        kernel,
        out_shape=(out, out, jax.ShapeDtypeStruct((2, SIMS, 128), F32)),
        in_specs=[hbm] * 5,
        out_specs=(vm, vm, vm),
        scratch_shapes=[
            pltpu.VMEM((NF, NM, NB, NS), BF16),
            pltpu.VMEM((NF, NM, NB, NB), BF16),
            pltpu.VMEM((256, 256), BF16),
            pltpu.VMEM((2, NY, TL, SIMS, HALF), BF16),
            pltpu.VMEM((2, 32, 16, 128), BF16),
            pltpu.VMEM((2, 31, 16, 128), BF16),
            pltpu.VMEM((NF, ROWS, NS), F32),
            pltpu.VMEM((NF, ROWS, NS), F32),
            slab, slab, slab, slab, wide, wide,
            pltpu.VMEM((NFQ, NF, F), F32),
            pltpu.VMEM((2, F * ROWS, F * ROWS), BF16),
            pltpu.VMEM((NF, NB), F32),
            pltpu.VMEM((2, 1, 128), F32),
            pltpu.VMEM((31, 1, 128), F32),
            pltpu.VMEM((7, 1, 128), F32),
            dma((NF,)), dma((5,)), dma((7,)), dma((7,)), dma((2, 3)), dma((2, 3)), dma, dma((2,)),
            dma((7,)), dma((7,)), dma((7,)), dma((7,)), dma((7,)), dma((7,)), dma, dma, dma, dma,
        ],
        compiler_params=pltpu.CompilerParams(
            collective_id=0, has_side_effects=True, vmem_limit_bytes=40 * 1024 * 1024),
    )(*[pltpu.with_memory_space_constraint(v, pltpu.HBM) for v in
        (visibilities, transfer, noise_weight, freq_prior, jnp.asarray(cas_table()))])
    step, ratio = coef[0, :, :1], coef[1, :, :1]
    residual = right - step * applied
    return step * right, residual, residual + ratio * right


def solution(mesh):
    return jax.shard_map(
        local,
        mesh=mesh,
        in_specs=(
            P("ma", "freq", None, None),
            P("freq", "ma", None, None),
            P("freq", None),
            P("freq", None),
        ),
        out_specs=(P("freq", "ma", None, None),) * 3,
        check_vma=False,
    )
```

time: 370 us -> 42.3 us (0.11)
  waiting for transfers between devices: 181 us -> 0 us
  blocking collectives: 150 us -> 0 us
  Pallas kernels: 0 us -> 40.6 us
  matrix products: 18.9 us -> 0 us
  between operations: 14.8 us -> 0.64 us
    unnamed x3 -> x0, waiting for transfers between devices: 153 us -> none
    psum x2 -> x0, blocking collectives: 150 us -> none  [the longest x1 76 us: local(): norm_now = lax.psum(local_norm, ('ma', 'freq'))]
    pallas_call x0 -> x1, Pallas kernels: none -> 40.6 us  [local(): pl.pallas_call(kernel, out_shape=(out, out, jax.ShapeDtypeStruct((2, SIMS...]
    all_gather x1 -> x0, waiting for transfers between devices: 27.8 us -> none  [local(): lax.all_gather(right_side, 'freq', axis=0, tiled=True)]
    dot_general x4 -> x0, matrix products: 18.9 us -> none  [the longest x1 9.35 us: local(): jnp.einsum('fmbs,fmkb->fmks', transfer, scaled, preferred_element_type=jn...]
  transfers between devices with their start and end apart: 2 -> 0, of which waited for: 2 -> 0; matrix products, arithmetic and copies ran while one was open for 0% -> 0% of each run, Pallas kernels for 0% -> 0%
where the time goes in v2:
time: 42.3 us
  Pallas kernels  40.6 us (96%)
  other arithmetic  0.89 us (2%)
  between operations  0.64 us (2%)
    pallas_call x1, Pallas kernels, local(): pl.pallas_call(kernel, out_shape=(out, out, jax.ShapeDtypeStruct((2, SIMS...  40.6 us
    add x1, other arithmetic, local(): return (step * right, residual, residual + ratio * right)  0.89 us

profile of v2, /device:TPU:1, one launch (start us, length us, event | category | flops | bytes accessed | tf_op | source)
XLA Modules:
  0.0 42.3 jit_solution(218564106460105537)
XLA Ops:
  0.6 40.6 %shard_map.76 = (f32[4,2,4,1024]{3,2,1,0:T(4,128)S(1)}, f32[4,2,4,1024]{3,2,1,0:T(4,128)S(1)}, f32[2,4,128]{2,1,0:T(4,128)S(1)}) custom-call(bf16[16,4,4,512]{3,2,1,0:T(4,128)(2,1)} %vis.1, bf16[4,2,512,1024]{3,2,1,0:T(8,128)(2,1)} %transfer.1, f32[4,512]{1,0:T(4,128)} %weight_hbm.1, f32[4,32]{1,0:T(4,128)} %prior_hbm.1, bf16[8,256,256]{2,1,0:T(8,128)(2,1)} %constant.2.clone.cas), custom_call_target="tpu_custom_call" | custom-call | tf_op jit(solution)/shard_map/pallas_call | solution.py:244
  41.2 0.1 slice_reduce_fusion
  41.4 0.9 %multiply_add_fusion = (f32[4,2,4,1024]{3,2,1,0:T(4,128)}, f32[4,2,4,1024]{3,2,1,0:T(4,128)}, f32[4,2,4,1024]{3,2,1,0:T(4,128)}) fusion(f32[4,2,4,1024]{3,2,1,0:T(4,128)S(1)} %get-tuple-element.7, f32[4]{0:T(128)S(1)} %get-tuple-element.9, f32[4,2,4,1024]{3,2,1,0:T(4,128)S(1)} %get-tuple-element.8, f32[4]{0:T(128)S(1)} %get-tuple-element.10), kind=kLoop, calls=%fused_computation | loop fusion | flops 163840 | bytes 655392 | tf_op jit(solution)/shard_map/add | solution.py:274

commit v3 on v2

--- a/solution.py
+++ b/solution.py
@@ -53,7 +53,7 @@
 
 def kernel(vis, transfer, weight_hbm, prior_hbm, cas, right_out, applied_out, coef_out,
            tv, gram, casv, vbuf, pbuf, rbuf, right, adj, rsl, rin, asl, ain, csl, cin, prior, spread, weight, dsend, d1, d2,
-           tsem, lsem, ps, pr, a1s, a1r, a2s, a2r, rs, rr, as_, ar, cs, cr, d1s, d1r, d2s, d2r):
+           tsem, lsem, ps, pr, a1s, a1r, a2s, a2r, rs, rr, as_, ar, cs, cr, d1s, d1r, d2s, d2r, round_sem):
     ma = lax.axis_index("ma")
     fq = lax.axis_index("freq")
     z, y = ma // NY, ma % NY
@@ -81,12 +81,17 @@
     for t in local_copies:
         t.start()
 
+    def greet(sem, ma_offsets, fq_offsets):
+        for o in ma_offsets:
+            pl.semaphore_signal(sem, 1, device_id=to_ma(*o))
+        for o in fq_offsets:
+            pl.semaphore_signal(sem, 1, device_id=to_fq(*o))
+
+    near = ([(1, 0), (NZ - 1, 0)], [(1, 0), (NX - 1, 0)])
     barrier = pltpu.get_barrier_semaphore()
-    for o in MA_OFFSETS:
-        pl.semaphore_signal(barrier, 1, device_id=to_ma(*o))
-    for o in FQ_OFFSETS:
-        pl.semaphore_signal(barrier, 1, device_id=to_fq(*o))
-    pl.semaphore_wait(barrier, len(MA_OFFSETS) + len(FQ_OFFSETS))
+    ys = [(0, dy) for dy in range(1, NY)]
+    greet(barrier, ys + near[0], near[1] + [(0, 1)])
+    pl.semaphore_wait(barrier, len(ys) + 5)
     pending = []
 
     def send(src, dst, ssem, rsem, peer):
@@ -97,10 +102,16 @@
 
     a1 = [[send(vis.at[:, lax.rem(y + dy, NY), :, halves[h]], vbuf.at[h, y], a1s.at[h, dy - 1], a1r.at[h, dy - 1],
                 to_ma(0, dy)) for dy in range(1, NY)] for h in range(2)]
-    pcs = [send(prior_hbm, prior.at[fq], ps.at[i], pr.at[i], to_fq(*o)) for i, o in enumerate(FQ_OFFSETS)]
+    greet(round_sem.at[0], *near)
     for t in tcopies:
         t.start()
+    pl.semaphore_wait(round_sem.at[0], 4)
+    greet(round_sem.at[1], [(2, 0), (NZ - 2, 0)], [(0, 1)])
+    pl.semaphore_wait(round_sem.at[1], 3)
+    greet(round_sem.at[2], near[0], [])
+    pcs = [send(prior_hbm, prior.at[fq], ps.at[i], pr.at[i], to_fq(*o)) for i, o in enumerate(FQ_OFFSETS)]
     cas_copy.wait()
+    pl.semaphore_wait(round_sem.at[2], 2)
 
     for h in range(2):
         own_vis[h].wait()
@@ -264,6 +275,7 @@
             pltpu.VMEM((7, 1, 128), F32),
             dma((NF,)), dma((5,)), dma((7,)), dma((7,)), dma((2, 3)), dma((2, 3)), dma, dma((2,)),
             dma((7,)), dma((7,)), dma((7,)), dma((7,)), dma((7,)), dma((7,)), dma, dma, dma, dma,
+            pltpu.SemaphoreType.REGULAR((3,)),
         ],
         compiler_params=pltpu.CompilerParams(
             collective_id=0, has_side_effects=True, vmem_limit_bytes=40 * 1024 * 1024),

time: 42.3 us -> 40.6 us (0.960)
  Pallas kernels: 40.6 us -> 38.8 us
    pallas_call x1, Pallas kernels: 40.6 us -> 38.8 us  [local(): pl.pallas_call(kernel, out_shape=(out, out, jax.ShapeDtypeStruct((2, SIMS...]
where the time goes in v3:
time: 40.6 us; the launch traced here: 40.5 us
  Pallas kernels  38.8 us (96%)
  other arithmetic  0.89 us (2%)
  between operations  0.64 us (2%)
    pallas_call x1, Pallas kernels, local(): pl.pallas_call(kernel, out_shape=(out, out, jax.ShapeDtypeStruct((2, SIMS...  38.8 us
    add x1, other arithmetic, local(): return (step * right, residual, residual + ratio * right)  0.89 us

profile of v3, /device:TPU:1, one launch (start us, length us, event | category | flops | bytes accessed | tf_op | source)
XLA Modules:
  0.0 40.5 jit_solution(12376760906484269292)
XLA Ops:
  0.6 38.8 %shard_map.76 = (f32[4,2,4,1024]{3,2,1,0:T(4,128)S(1)}, f32[4,2,4,1024]{3,2,1,0:T(4,128)S(1)}, f32[2,4,128]{2,1,0:T(4,128)S(1)}) custom-call(bf16[16,4,4,512]{3,2,1,0:T(4,128)(2,1)} %vis.1, bf16[4,2,512,1024]{3,2,1,0:T(8,128)(2,1)} %transfer.1, f32[4,512]{1,0:T(4,128)} %weight_hbm.1, f32[4,32]{1,0:T(4,128)} %prior_hbm.1, bf16[8,256,256]{2,1,0:T(8,128)(2,1)} %constant.2.clone.cas), custom_call_target="tpu_custom_call" | custom-call | tf_op jit(solution)/shard_map/pallas_call | solution.py:255
  39.5 0.1 slice_reduce_fusion
  39.6 0.9 %multiply_add_fusion = (f32[4,2,4,1024]{3,2,1,0:T(4,128)}, f32[4,2,4,1024]{3,2,1,0:T(4,128)}, f32[4,2,4,1024]{3,2,1,0:T(4,128)}) fusion(f32[4,2,4,1024]{3,2,1,0:T(4,128)S(1)} %get-tuple-element.7, f32[4]{0:T(128)S(1)} %get-tuple-element.9, f32[4,2,4,1024]{3,2,1,0:T(4,128)S(1)} %get-tuple-element.8, f32[4]{0:T(128)S(1)} %get-tuple-element.10), kind=kLoop, calls=%fused_computation | loop fusion | flops 163840 | bytes 655392 | tf_op jit(solution)/shard_map/add | solution.py:286

commit v4 on v3

--- a/solution.py
+++ b/solution.py
@@ -18,7 +18,8 @@
 HALF = NB // 2
 F32, BF16 = jnp.float32, jnp.bfloat16
 HIGH = lax.Precision.HIGHEST
-MA_OFFSETS = [(dz, dy) for dz in range(NZ) for dy in range(NY) if dz or dy]
+MA_GROUPS = [[(dz, dy) for dz in zs for dy in (2, 1, 3, 0) if dz or dy] for zs in ((3, 5, 1, 7), (4, 2, 6, 0))]
+MA_OFFSETS = MA_GROUPS[1] + MA_GROUPS[0]
 FQ_OFFSETS = [(dx, dc) for dx in range(NX) for dc in range(NC) if dx or dc]
 
 
@@ -28,10 +29,10 @@
     arg = (m[:, None] * t[None, :]) % NT
     ang = arg.astype(np.float32) * np.float32(2.0 * math.pi / NT)
     cas = (np.cos(ang) + np.sin(ang)) * np.float32(1.0 / math.sqrt(NT))
-    cas = cas.reshape(64, NZ, 64).transpose(1, 0, 2)
+    cas = cas.reshape(64, NZ // 2, 128).transpose(1, 0, 2)
     eye = np.eye(SIMS, dtype=np.float32)
     full = cas[:, :, None, :, None] * eye[None, None, :, None, :]
-    return full.reshape(NZ, 256, 256).astype(jnp.bfloat16)
+    return full.reshape(NZ // 2, 256, 512).astype(jnp.bfloat16)
 
 
 def dot(a, b, **kw):
@@ -51,12 +52,13 @@
     return sum(v[:, i * 128:(i + 1) * 128] for i in range(NS // 128))
 
 
-def kernel(vis, transfer, weight_hbm, prior_hbm, cas, right_out, applied_out, coef_out,
-           tv, gram, casv, vbuf, pbuf, rbuf, right, adj, rsl, rin, asl, ain, csl, cin, prior, spread, weight, dsend, d1, d2,
+def kernel(vis, transfer, weight_hbm, prior_hbm, cas, right_out, applied_out, step_out, ratio_out,
+           tv, turned, casv, vbuf, pbuf, rbuf0, rbuf1, right, adj, rsl, rin, asl, ain, csl, cin, prior, spread, weight, dsend, d1, d2,
            tsem, lsem, ps, pr, a1s, a1r, a2s, a2r, rs, rr, as_, ar, cs, cr, d1s, d1r, d2s, d2r, round_sem):
     ma = lax.axis_index("ma")
     fq = lax.axis_index("freq")
     z, y = ma // NY, ma % NY
+    rbuf = (rbuf0, rbuf1)
     x, c = fq // NC, fq % NC
 
     def ma_peer(dz, dy):
@@ -72,9 +74,15 @@
         return {"ma": ma, "freq": fq_peer(dx, dc)}
 
     tcopies = [pltpu.make_async_copy(transfer.at[f], tv.at[f], tsem.at[f]) for f in range(NF)]
-    halves = [pl.ds(h * HALF, HALF) for h in range(2)]
-    cas_copy = pltpu.make_async_copy(cas.at[z], casv, lsem.at[0])
-    own_vis = [pltpu.make_async_copy(vis.at[:, y, :, halves[h]], vbuf.at[h, y], lsem.at[1 + h]) for h in range(2)]
+    odd = z % 2
+    mate = z + 1 - 2 * odd
+    other = lax.rem(z + NZ - 1 + 2 * odd, NZ)
+
+    def half(h):
+        return pl.ds(pl.multiple_of(h * HALF, HALF), HALF)
+
+    cas_copy = pltpu.make_async_copy(cas.at[z // 2], casv, lsem.at[0])
+    own_vis = [pltpu.make_async_copy(vis.at[:, y, :, half(odd)], vbuf.at[odd, y], lsem.at[1])]
     own_prior = pltpu.make_async_copy(prior_hbm, prior.at[fq], lsem.at[3])
     own_weight = pltpu.make_async_copy(weight_hbm, weight, lsem.at[4])
     local_copies = [*own_vis, cas_copy, own_prior, own_weight]
@@ -87,11 +95,16 @@
         for o in fq_offsets:
             pl.semaphore_signal(sem, 1, device_id=to_fq(*o))
 
+    def at_z(zz, dy):
+        return {"ma": zz * NY + lax.rem(y + dy, NY), "freq": fq}
+
     near = ([(1, 0), (NZ - 1, 0)], [(1, 0), (NX - 1, 0)])
+    pair = [at_z(mate, dy) for dy in range(NY)] + [at_z(z, dy) for dy in range(1, NY)]
     barrier = pltpu.get_barrier_semaphore()
-    ys = [(0, dy) for dy in range(1, NY)]
-    greet(barrier, ys + near[0], near[1] + [(0, 1)])
-    pl.semaphore_wait(barrier, len(ys) + 5)
+    for peer in pair + [at_z(other, 0)]:
+        pl.semaphore_signal(barrier, 1, device_id=peer)
+    greet(barrier, [], near[1] + [(0, 1)])
+    pl.semaphore_wait(barrier, len(pair) + 4)
     pending = []
 
     def send(src, dst, ssem, rsem, peer):
@@ -100,8 +113,9 @@
         pending.append(copy)
         return copy
 
-    a1 = [[send(vis.at[:, lax.rem(y + dy, NY), :, halves[h]], vbuf.at[h, y], a1s.at[h, dy - 1], a1r.at[h, dy - 1],
-                to_ma(0, dy)) for dy in range(1, NY)] for h in range(2)]
+    a1 = []
+    for i, (peer, h, dy) in enumerate([(at_z(mate, dy), 1 - odd, dy) for dy in range(NY)] + [(at_z(z, dy), odd, dy) for dy in range(1, NY)]):
+        a1.append(send(vis.at[:, lax.rem(y + dy, NY), :, half(h)], vbuf.at[odd, y], a1s.at[i], a1r.at[i], peer))
     greet(round_sem.at[0], *near)
     for t in tcopies:
         t.start()
@@ -113,14 +127,14 @@
     cas_copy.wait()
     pl.semaphore_wait(round_sem.at[2], 2)
 
+    own_vis[0].wait()
+    for r in a1:
+        r.wait_recv()
+    part = dot(casv[...], vbuf[...].reshape(512, HALF)).reshape(32, ROWS, HALF)
+    pbuf[...] = jnp.concatenate([part[:, :, :128], part[:, :, 128:]], axis=1).astype(BF16)
     for h in range(2):
-        own_vis[h].wait()
-        for r in a1[h]:
-            r.wait_recv()
-        part = dot(casv[...], vbuf[h].reshape(256, HALF)).reshape(32, ROWS, HALF)
-        pbuf[h] = jnp.concatenate([part[:, :, :128], part[:, :, 128:]], axis=1).astype(BF16)
-        for dz, dy in MA_OFFSETS:
-            send(pbuf.at[h, ma_peer(dz, dy)], rbuf.at[h, dz * NY + dy - 1], a2s, a2r.at[h], to_ma(dz, dy))
+        for i, o in enumerate(MA_GROUPS[h]):
+            send(pbuf.at[ma_peer(*o)], rbuf[h].at[i], a2s, a2r.at[h], to_ma(*o))
 
     own_prior.wait()
     own_weight.wait()
@@ -139,31 +153,27 @@
     @pl.loop(0, NF)
     def _(f):
         for m in range(NM):
-            block = tv[f, m]
-            gram[f, m] = dot_t(block, block).astype(BF16)
+            turned[f, m] = tv[f, m].T
 
     low = iota((ROWS, 1), 0) < SIMS
 
     def both(a, ref, f, at=slice(None)):
         return jnp.where(low, dot(a, ref[f, 0, at]), dot(a, ref[f, 1, at]))
 
-    acc, obs = [None] * NY, [None] * NY
+    acc = [None] * NY
     for h in range(2):
-        pltpu.make_async_copy(rbuf.at[h], rbuf.at[h], a2r.at[h]).wait()
+        pltpu.make_async_copy(rbuf[h], rbuf[h], a2r.at[h]).wait()
+        rows = half(1 - odd if h == 0 else odd)
         for dy in range(NY):
             f = lax.rem(y + NY - dy, NY)
-            total = None
-            for dz in range(NZ):
-                slot = dz * NY + dy
-                piece = pbuf[h, ma] if slot == 0 else rbuf[h, slot - 1]
-                piece = piece.astype(F32)
-                total = piece if total is None else total + piece
+            pieces = [rbuf[h][i] for i, o in enumerate(MA_GROUPS[h]) if o[1] == dy]
+            if h == 1 and dy == 0:
+                pieces.append(pbuf[ma])
+            total = sum(p.astype(F32) for p in pieces)
             modes = jnp.concatenate([total[:ROWS], total[ROWS:]], axis=1)
-            weighted = (weight[pl.ds(f, 1), halves[h]] * modes).astype(BF16)
-            out = both(weighted, tv, f, halves[h])
+            weighted = (weight[pl.ds(f, 1), rows] * modes).astype(BF16)
+            out = both(weighted, tv, f, rows)
             acc[dy] = out if h == 0 else acc[dy] + out
-            out = both(weighted, gram, f, halves[h])
-            obs[dy] = out if h == 0 else obs[dy] + out
     for dy in range(NY):
         right[lax.rem(y + NY - dy, NY)] = acc[dy]
 
@@ -179,7 +189,8 @@
 
     for dy in range(NY):
         f = lax.rem(y + NY - dy, NY)
-        scaled = (weight[pl.ds(f, 1), :] * obs[dy]).astype(BF16)
+        observed = both(acc[dy].astype(BF16), turned, f)
+        scaled = (weight[pl.ds(f, 1), :] * observed).astype(BF16)
         adj[f] = both(scaled, tv, f)
     at = adj[...].reshape(OWN, NS)
     slices(at, asl)
@@ -198,19 +209,18 @@
     def blocks(v):
         return sum(v[i * ROWS:(i + 1) * ROWS] for i in range(F))
 
-    n = lane_tiles(rt * rt)
-    cu = lane_tiles(rt * at) + blocks(rall.astype(F32) * coupled)
-    q = lane_tiles(at * at)
-    for r in ac:
-        r.wait_recv()
-    q = q + blocks((2.0 * ain[...].reshape(F * ROWS, LANES).astype(F32) + coupled) * coupled)
-
     row, lane = iota((ROWS, 128), 0), iota((ROWS, 128), 1)
 
     def put(v, at_lane):
         return jnp.where(lane == row + at_lane, jnp.sum(v, axis=1, keepdims=True), 0.0)
 
-    own = jnp.sum(put(n, 0) + put(cu, ROWS) + put(q, 2 * ROWS), axis=0, keepdims=True)
+    rest = put(lane_tiles(rt * rt), 0) + put(lane_tiles(rt * at) + blocks(rall.astype(F32) * coupled), ROWS)
+    image = lane_tiles(at * at) + blocks(coupled * coupled)
+    for r in ac:
+        r.wait_recv()
+    image = image + blocks(2.0 * ain[...].reshape(F * ROWS, LANES).astype(F32) * coupled)
+
+    own = jnp.sum(rest + put(image, 2 * ROWS), axis=0, keepdims=True)
     dsend[0] = own
     for i, o in enumerate(MA_OFFSETS):
         send(dsend.at[0], d1.at[i], d1s, d1r, to_ma(*o))
@@ -239,8 +249,8 @@
     norm, curve, image = take(0), take(ROWS), take(2 * ROWS)
     step = norm / curve
     ratio = (image / curve) * step - 1.0
-    coef_out[0] = jnp.broadcast_to(step[:SIMS], (SIMS, 128))
-    coef_out[1] = jnp.broadcast_to(ratio[:SIMS], (SIMS, 128))
+    step_out[...] = jnp.broadcast_to(step[:SIMS], (SIMS, NS))
+    ratio_out[...] = jnp.broadcast_to(ratio[:SIMS], (SIMS, NS))
     for r in pending:
         r.wait_send()
 
@@ -250,20 +260,22 @@
     hbm = pl.BlockSpec(memory_space=pltpu.HBM)
     dma = pltpu.SemaphoreType.DMA
     out = jax.ShapeDtypeStruct((NF, NM, SIMS, NS), F32)
+    coef = jax.ShapeDtypeStruct((SIMS, NS), F32)
     slab = pltpu.VMEM((NFQ, OWN, LANES), BF16)
     wide = pltpu.VMEM((NFQ, OWN, LANES), F32)
-    right, applied, coef = pl.pallas_call(
+    right, applied, step, ratio = pl.pallas_call(
         kernel,
-        out_shape=(out, out, jax.ShapeDtypeStruct((2, SIMS, 128), F32)),
+        out_shape=(out, out, coef, coef),
         in_specs=[hbm] * 5,
-        out_specs=(vm, vm, vm),
+        out_specs=(vm,) * 4,
         scratch_shapes=[
             pltpu.VMEM((NF, NM, NB, NS), BF16),
-            pltpu.VMEM((NF, NM, NB, NB), BF16),
-            pltpu.VMEM((256, 256), BF16),
+            pltpu.VMEM((NF, NM, NS, NB), BF16),
+            pltpu.VMEM((256, 512), BF16),
             pltpu.VMEM((2, NY, TL, SIMS, HALF), BF16),
-            pltpu.VMEM((2, 32, 16, 128), BF16),
-            pltpu.VMEM((2, 31, 16, 128), BF16),
+            pltpu.VMEM((32, 16, 128), BF16),
+            pltpu.VMEM((16, 16, 128), BF16),
+            pltpu.VMEM((15, 16, 128), BF16),
             pltpu.VMEM((NF, ROWS, NS), F32),
             pltpu.VMEM((NF, ROWS, NS), F32),
             slab, slab, slab, slab, wide, wide,
@@ -273,7 +285,7 @@
             pltpu.VMEM((2, 1, 128), F32),
             pltpu.VMEM((31, 1, 128), F32),
             pltpu.VMEM((7, 1, 128), F32),
-            dma((NF,)), dma((5,)), dma((7,)), dma((7,)), dma((2, 3)), dma((2, 3)), dma, dma((2,)),
+            dma((NF,)), dma((5,)), dma((7,)), dma((7,)), dma((7,)), dma((7,)), dma, dma((2,)),
             dma((7,)), dma((7,)), dma((7,)), dma((7,)), dma((7,)), dma((7,)), dma, dma, dma, dma,
             pltpu.SemaphoreType.REGULAR((3,)),
         ],
@@ -281,7 +293,6 @@
             collective_id=0, has_side_effects=True, vmem_limit_bytes=40 * 1024 * 1024),
     )(*[pltpu.with_memory_space_constraint(v, pltpu.HBM) for v in
         (visibilities, transfer, noise_weight, freq_prior, jnp.asarray(cas_table()))])
-    step, ratio = coef[0, :, :1], coef[1, :, :1]
     residual = right - step * applied
     return step * right, residual, residual + ratio * right
 

time: 40.6 us -> 39.9 us (0.983)
    pallas_call x1, Pallas kernels: 38.8 us -> 38.4 us  [local(): pl.pallas_call(kernel, out_shape=(out, out, coef, coef), in_specs=[hbm] *...]
where the time goes in v4:
time: 39.9 us; the launch traced here: 39.8 us
  Pallas kernels  38.4 us (96%)
  other arithmetic  0.77 us (2%)
  between operations  0.65 us (2%)
    pallas_call x1, Pallas kernels, local(): pl.pallas_call(kernel, out_shape=(out, out, coef, coef), in_specs=[hbm] *...  38.4 us

profile of v4, /device:TPU:1, one launch (start us, length us, event | category | flops | bytes accessed | tf_op | source)
XLA Modules:
  0.0 39.8 jit_solution(7966815061201078239)
XLA Ops:
  0.6 38.4 %shard_map.76 = (f32[4,2,4,1024]{3,2,1,0:T(4,128)S(1)}, f32[4,2,4,1024]{3,2,1,0:T(4,128)S(1)}, f32[4,1024]{1,0:T(4,128)S(1)}, f32[4,1024]{1,0:T(4,128)S(1)}) custom-call(bf16[16,4,4,512]{3,2,1,0:T(4,128)(2,1)} %vis.1, bf16[4,2,512,1024]{3,2,1,0:T(8,128)(2,1)} %transfer.1, f32[4,512]{1,0:T(4,128)} %weight_hbm.1, f32[4,32]{1,0:T(4,128)} %prior_hbm.1, ...), custom_call_target="tpu_custom_call" | custom-call | tf_op jit(solution)/shard_map/pallas_call | solution.py:266
  39.0 0.8 %multiply_add_fusion = (f32[4,1,8,1024]{3,2,1,0:T(8,128)}, f32[4,1,8,1024]{3,2,1,0:T(8,128)}, f32[4,1,8,1024]{3,2,1,0:T(8,128)}) fusion(f32[4,1,8,1024]{3,2,1,0:T(8,128)S(1)} %bitcast.7, f32[8,1024]{1,0:T(8,128)S(1)} %bitcast.10, f32[4,1,8,1024]{3,2,1,0:T(8,128)S(1)} %bitcast.8, f32[8,1024]{1,0:T(8,128)S(1)} %bitcast.9), kind=kLoop, calls=%fused_computation | loop fusion | flops 163840 | bytes 720896 | tf_op jit(solution)/shard_map/add | solution.py:297
  (2 shorter events, 0.0 us)

commit v5 on v4

--- a/solution.py
+++ b/solution.py
@@ -19,7 +19,7 @@
 F32, BF16 = jnp.float32, jnp.bfloat16
 HIGH = lax.Precision.HIGHEST
 MA_GROUPS = [[(dz, dy) for dz in zs for dy in (2, 1, 3, 0) if dz or dy] for zs in ((3, 5, 1, 7), (4, 2, 6, 0))]
-MA_OFFSETS = MA_GROUPS[1] + MA_GROUPS[0]
+MA_OFFSETS = sorted(MA_GROUPS[0] + MA_GROUPS[1], key=lambda o: -min(o[0], NZ - o[0]) - min(o[1], NY - o[1]))
 FQ_OFFSETS = [(dx, dc) for dx in range(NX) for dc in range(NC) if dx or dc]
 
 
@@ -86,8 +86,6 @@
     own_prior = pltpu.make_async_copy(prior_hbm, prior.at[fq], lsem.at[3])
     own_weight = pltpu.make_async_copy(weight_hbm, weight, lsem.at[4])
     local_copies = [*own_vis, cas_copy, own_prior, own_weight]
-    for t in local_copies:
-        t.start()
 
     def greet(sem, ma_offsets, fq_offsets):
         for o in ma_offsets:
@@ -104,6 +102,8 @@
     for peer in pair + [at_z(other, 0)]:
         pl.semaphore_signal(barrier, 1, device_id=peer)
     greet(barrier, [], near[1] + [(0, 1)])
+    for t in local_copies + tcopies:
+        t.start()
     pl.semaphore_wait(barrier, len(pair) + 4)
     pending = []
 
@@ -113,12 +113,16 @@
         pending.append(copy)
         return copy
 
+    def drain():
+        for copy in pending:
+            copy.wait_send()
+        pending.clear()
+
     a1 = []
-    for i, (peer, h, dy) in enumerate([(at_z(mate, dy), 1 - odd, dy) for dy in range(NY)] + [(at_z(z, dy), odd, dy) for dy in range(1, NY)]):
+    for i, (peer, h, dy) in enumerate([(at_z(mate, 2), 1 - odd, 2), (at_z(z, 2), odd, 2), (at_z(mate, 1), 1 - odd, 1), (at_z(mate, 3), 1 - odd, 3),
+                                              (at_z(z, 1), odd, 1), (at_z(z, 3), odd, 3), (at_z(mate, 0), 1 - odd, 0)]):
         a1.append(send(vis.at[:, lax.rem(y + dy, NY), :, half(h)], vbuf.at[odd, y], a1s.at[i], a1r.at[i], peer))
     greet(round_sem.at[0], *near)
-    for t in tcopies:
-        t.start()
     pl.semaphore_wait(round_sem.at[0], 4)
     greet(round_sem.at[1], [(2, 0), (NZ - 2, 0)], [(0, 1)])
     pl.semaphore_wait(round_sem.at[1], 3)
@@ -134,7 +138,7 @@
     pbuf[...] = jnp.concatenate([part[:, :, :128], part[:, :, 128:]], axis=1).astype(BF16)
     for h in range(2):
         for i, o in enumerate(MA_GROUPS[h]):
-            send(pbuf.at[ma_peer(*o)], rbuf[h].at[i], a2s, a2r.at[h], to_ma(*o))
+            pltpu.make_async_remote_copy(pbuf.at[ma_peer(*o)], rbuf[h].at[i], a2s.at[h], a2r.at[h], device_id=to_ma(*o)).start()
 
     own_prior.wait()
     own_weight.wait()
@@ -202,31 +206,35 @@
     rall = rin[...].reshape(F * ROWS, LANES)
     coupled = dot(spread[...].reshape(2 * F * ROWS, F * ROWS), rall)
     coupled = coupled[:F * ROWS] + coupled[F * ROWS:]
+
+    def blocks(v):
+        return sum(v[i * ROWS:(i + 1) * ROWS] for i in range(F))
+
+    row, lane = iota((ROWS, 128), 0), iota((ROWS, 128), 1)
+
+    def put(v, at_lane):
+        return jnp.where(lane == row + at_lane, jnp.sum(v, axis=1, keepdims=True), 0.0)
+
+    rest = put(lane_tiles(rt * rt), 0) + put(lane_tiles(rt * at) + blocks(rall.astype(F32) * coupled), ROWS)
+    image = lane_tiles(at * at) + blocks(coupled * coupled)
+    for r in ac:
+        r.wait_recv()
+    image = image + blocks(2.0 * ain[...].reshape(F * ROWS, LANES).astype(F32) * coupled)
+
+    own = jnp.sum(rest + put(image, 2 * ROWS), axis=0, keepdims=True)
+    dsend[0] = own
+    for i, o in enumerate(MA_OFFSETS):
+        pltpu.make_async_remote_copy(dsend.at[0], d1.at[i], d1s, d1r, device_id=to_ma(*o)).start()
     csl[...] = coupled.reshape(NFQ, OWN, LANES)
     cc = [send(csl.at[fq_peer(*o)], cin.at[fq], cs.at[i], cr.at[i], to_fq(*o)) for i, o in enumerate(FQ_OFFSETS)]
     cin[fq] = csl[fq]
-
-    def blocks(v):
-        return sum(v[i * ROWS:(i + 1) * ROWS] for i in range(F))
-
-    row, lane = iota((ROWS, 128), 0), iota((ROWS, 128), 1)
-
-    def put(v, at_lane):
-        return jnp.where(lane == row + at_lane, jnp.sum(v, axis=1, keepdims=True), 0.0)
-
-    rest = put(lane_tiles(rt * rt), 0) + put(lane_tiles(rt * at) + blocks(rall.astype(F32) * coupled), ROWS)
-    image = lane_tiles(at * at) + blocks(coupled * coupled)
-    for r in ac:
-        r.wait_recv()
-    image = image + blocks(2.0 * ain[...].reshape(F * ROWS, LANES).astype(F32) * coupled)
-
-    own = jnp.sum(rest + put(image, 2 * ROWS), axis=0, keepdims=True)
-    dsend[0] = own
-    for i, o in enumerate(MA_OFFSETS):
-        send(dsend.at[0], d1.at[i], d1s, d1r, to_ma(*o))
     for f in range(NF):
         for m in range(NM):
             right_out[f, m] = right[f, m * SIMS:(m + 1) * SIMS]
+    drain()
+    for h in range(2):
+        pltpu.make_async_copy(rbuf[h], rbuf[h], a2s.at[h]).wait()
+    pltpu.make_async_copy(d1, d1, d1s).wait()
     pltpu.make_async_copy(d1, d1, d1r).wait()
     own = own + jnp.sum(d1[...], axis=0)
     dsend[1] = own
@@ -251,8 +259,7 @@
     ratio = (image / curve) * step - 1.0
     step_out[...] = jnp.broadcast_to(step[:SIMS], (SIMS, NS))
     ratio_out[...] = jnp.broadcast_to(ratio[:SIMS], (SIMS, NS))
-    for r in pending:
-        r.wait_send()
+    drain()
 
 
 def local(visibilities, transfer, noise_weight, freq_prior):
@@ -285,7 +292,7 @@
             pltpu.VMEM((2, 1, 128), F32),
             pltpu.VMEM((31, 1, 128), F32),
             pltpu.VMEM((7, 1, 128), F32),
-            dma((NF,)), dma((5,)), dma((7,)), dma((7,)), dma((7,)), dma((7,)), dma, dma((2,)),
+            dma((NF,)), dma((5,)), dma((7,)), dma((7,)), dma((7,)), dma((7,)), dma((2,)), dma((2,)),
             dma((7,)), dma((7,)), dma((7,)), dma((7,)), dma((7,)), dma((7,)), dma, dma, dma, dma,
             pltpu.SemaphoreType.REGULAR((3,)),
         ],

time: 39.9 us -> 39.6 us (level)
  no operation moved by 1% of the time
where the time goes in v5:
time: 39.6 us; the launch traced here: 39.5 us
  Pallas kernels  38.1 us (96%)
  other arithmetic  0.77 us (2%)
  between operations  0.65 us (2%)
    pallas_call x1, Pallas kernels, local(): pl.pallas_call(kernel, out_shape=(out, out, coef, coef), in_specs=[hbm] *...  38.1 us

profile of v5, /device:TPU:1, one launch (start us, length us, event | category | flops | bytes accessed | tf_op | source)
XLA Modules:
  0.0 39.5 jit_solution(4306522662100657073)
XLA Ops:
  0.6 38.1 %shard_map.76 = (f32[4,2,4,1024]{3,2,1,0:T(4,128)S(1)}, f32[4,2,4,1024]{3,2,1,0:T(4,128)S(1)}, f32[4,1024]{1,0:T(4,128)S(1)}, f32[4,1024]{1,0:T(4,128)S(1)}) custom-call(bf16[16,4,4,512]{3,2,1,0:T(4,128)(2,1)} %vis.1, bf16[4,2,512,1024]{3,2,1,0:T(8,128)(2,1)} %transfer.1, f32[4,512]{1,0:T(4,128)} %weight_hbm.1, f32[4,32]{1,0:T(4,128)} %prior_hbm.1, ...), custom_call_target="tpu_custom_call" | custom-call | tf_op jit(solution)/shard_map/pallas_call | solution.py:273
  38.7 0.8 %multiply_add_fusion = (f32[4,1,8,1024]{3,2,1,0:T(8,128)}, f32[4,1,8,1024]{3,2,1,0:T(8,128)}, f32[4,1,8,1024]{3,2,1,0:T(8,128)}) fusion(f32[4,1,8,1024]{3,2,1,0:T(8,128)S(1)} %bitcast.7, f32[8,1024]{1,0:T(8,128)S(1)} %bitcast.10, f32[4,1,8,1024]{3,2,1,0:T(8,128)S(1)} %bitcast.8, f32[8,1024]{1,0:T(8,128)S(1)} %bitcast.9), kind=kLoop, calls=%fused_computation | loop fusion | flops 163840 | bytes 720896 | tf_op jit(solution)/shard_map/add | solution.py:304
  (2 shorter events, 0.0 us)

commit v6 on v5

--- a/solution.py
+++ b/solution.py
@@ -223,23 +223,21 @@
 
     own = jnp.sum(rest + put(image, 2 * ROWS), axis=0, keepdims=True)
     dsend[0] = own
+    for i, o in enumerate(FQ_OFFSETS):
+        send(dsend.at[0], d2.at[i], d2s, d2r, to_fq(*o))
+    for f in range(NF):
+        for m in range(NM):
+            right_out[f, m] = right[f, m * SIMS:(m + 1) * SIMS]
+    for h in range(2):
+        pltpu.make_async_copy(rbuf[h], rbuf[h], a2s.at[h]).wait()
+    pltpu.make_async_copy(d2, d2, d2r).wait()
+    own = own + jnp.sum(d2[...], axis=0)
+    dsend[1] = own
     for i, o in enumerate(MA_OFFSETS):
-        pltpu.make_async_remote_copy(dsend.at[0], d1.at[i], d1s, d1r, device_id=to_ma(*o)).start()
+        pltpu.make_async_remote_copy(dsend.at[1], d1.at[i], d1s, d1r, device_id=to_ma(*o)).start()
     csl[...] = coupled.reshape(NFQ, OWN, LANES)
     cc = [send(csl.at[fq_peer(*o)], cin.at[fq], cs.at[i], cr.at[i], to_fq(*o)) for i, o in enumerate(FQ_OFFSETS)]
     cin[fq] = csl[fq]
-    for f in range(NF):
-        for m in range(NM):
-            right_out[f, m] = right[f, m * SIMS:(m + 1) * SIMS]
-    drain()
-    for h in range(2):
-        pltpu.make_async_copy(rbuf[h], rbuf[h], a2s.at[h]).wait()
-    pltpu.make_async_copy(d1, d1, d1s).wait()
-    pltpu.make_async_copy(d1, d1, d1r).wait()
-    own = own + jnp.sum(d1[...], axis=0)
-    dsend[1] = own
-    for i, o in enumerate(FQ_OFFSETS):
-        send(dsend.at[1], d2.at[i], d2s, d2r, to_fq(*o))
     for r in cc:
         r.wait_recv()
     for f in range(NF):
@@ -247,8 +245,10 @@
         applied = adj[f] + coup
         for m in range(NM):
             applied_out[f, m] = applied[m * SIMS:(m + 1) * SIMS]
-    pltpu.make_async_copy(d2, d2, d2r).wait()
-    own = own + jnp.sum(d2[...], axis=0)
+    drain()
+    pltpu.make_async_copy(d1, d1, d1s).wait()
+    pltpu.make_async_copy(d1, d1, d1r).wait()
+    own = own + jnp.sum(d1[...], axis=0)
 
     def take(at_lane):
         inside = (lane >= at_lane) & (lane < at_lane + ROWS) & (lane % SIMS == row % SIMS)

time: 39.6 us -> 39.3 us (level)
  no operation moved by 1% of the time
where the time goes in v6:
time: 39.3 us; the launch traced here: 39.2 us
  Pallas kernels  37.8 us (96%)
  other arithmetic  0.77 us (2%)
  between operations  0.65 us (2%)
    pallas_call x1, Pallas kernels, local(): pl.pallas_call(kernel, out_shape=(out, out, coef, coef), in_specs=[hbm] *...  37.8 us

profile of v6, /device:TPU:1, one launch (start us, length us, event | category | flops | bytes accessed | tf_op | source)
XLA Modules:
  0.0 39.2 jit_solution(16243413486756252700)
XLA Ops:
  0.6 37.8 %shard_map.76 = (f32[4,2,4,1024]{3,2,1,0:T(4,128)S(1)}, f32[4,2,4,1024]{3,2,1,0:T(4,128)S(1)}, f32[4,1024]{1,0:T(4,128)S(1)}, f32[4,1024]{1,0:T(4,128)S(1)}) custom-call(bf16[16,4,4,512]{3,2,1,0:T(4,128)(2,1)} %vis.1, bf16[4,2,512,1024]{3,2,1,0:T(8,128)(2,1)} %transfer.1, f32[4,512]{1,0:T(4,128)} %weight_hbm.1, f32[4,32]{1,0:T(4,128)} %prior_hbm.1, ...), custom_call_target="tpu_custom_call" | custom-call | tf_op jit(solution)/shard_map/pallas_call | solution.py:273
  38.4 0.8 %multiply_add_fusion = (f32[4,1,8,1024]{3,2,1,0:T(8,128)}, f32[4,1,8,1024]{3,2,1,0:T(8,128)}, f32[4,1,8,1024]{3,2,1,0:T(8,128)}) fusion(f32[4,1,8,1024]{3,2,1,0:T(8,128)S(1)} %bitcast.7, f32[8,1024]{1,0:T(8,128)S(1)} %bitcast.10, f32[4,1,8,1024]{3,2,1,0:T(8,128)S(1)} %bitcast.8, f32[8,1024]{1,0:T(8,128)S(1)} %bitcast.9), kind=kLoop, calls=%fused_computation | loop fusion | flops 163840 | bytes 720896 | tf_op jit(solution)/shard_map/add | solution.py:304
  (2 shorter events, 0.0 us)
